TPU v7x, 32 devices: a whole 2x2x4 slice. The times are simulated.
32 devices in a mesh: seq: 8 (over z, y), ch: 4 (over x, core).
Axes of the slice: x: 2, y: 2, z: 4, core: 2. Of those that a mesh axis runs over, the one named last changes fastest.
Arguments:
- query_rows: bfloat16 [2048, 4096], P(('seq', 'ch')), may hold values from -6 to 6
- key_rows: bfloat16 [2048, 4096], P(('seq', 'ch')), may hold values from -6 to 6
- value_rows: bfloat16 [2048, 4096], P(('seq', 'ch')), may hold values from -6 to 6
- filter_taps: float32 [2048, 4096], P(('seq', 'ch')), may hold values from -1.1 to 1.1
- skip_gain: float32 [4096], replicated, may hold values from 0.5 to 1.5
Outputs:
- gated_output: bfloat16 [2048, 4096], P(('seq', 'ch'))
All inputs are finite; a program needn't handle non-finite values.
Results may differ from a plain program's by a relative error of at most 0.0014.
Values sent between devices are 32-bit elements; how exact they have to be, the bound alone decides.
A program may use at most 128 MiB of HBM per device.

v0:
```python
import math
import jax
import jax.numpy as jnp
from jax import lax
from jax.sharding import PartitionSpec as P

highest = lax.Precision.HIGHEST


def angles(product_ids, modulus):
    return 2.0 * math.pi / modulus * (product_ids % modulus).astype(jnp.float32)


def contract(pattern, weights, operand):
    return jnp.einsum(
        pattern, weights, operand, precision=highest, preferred_element_type=jnp.float32
    )


def shards(query_rows, key_rows, value_rows, filter_taps, skip_gain):
    seq_count = lax.axis_size("seq")
    group_count = lax.axis_size("ch")
    position = lax.axis_index("seq")
    row_count, full_width = key_rows.shape
    per_peer = row_count // seq_count
    columns = full_width // group_count
    local_rows = group_count * per_peer
    tokens = row_count * group_count
    slot_count = 2 * seq_count
    length = 2 * tokens * seq_count
    signal = key_rows.astype(jnp.float32) * value_rows.astype(jnp.float32)
    layout = (1, seq_count, 1, per_peer, full_width)
    moved_signal, moved_filter = (
        lax.all_to_all(
            lax.all_to_all(signal.reshape(layout), "seq", split_axis=1, concat_axis=0, tiled=True),
            "ch",
            split_axis=4,
            concat_axis=2,
            tiled=True,
        ),
        lax.all_to_all(
            lax.all_to_all(
                filter_taps.reshape(layout), "seq", split_axis=1, concat_axis=0, tiled=True
            ),
            "ch",
            split_axis=4,
            concat_axis=2,
            tiled=True,
        ),
    )
    moved_signal = moved_signal.reshape(seq_count, local_rows, columns)
    moved_filter = moved_filter.reshape(seq_count, local_rows, columns)
    slot_ids = jnp.arange(slot_count, dtype=jnp.int32)
    owners = slot_ids // 2
    freq_slot = jnp.where(
        slot_ids % 2 == 0, owners, jnp.where(owners == 0, seq_count, slot_count - owners)
    )
    blocks = jnp.arange(seq_count, dtype=jnp.int32)
    block_phase = angles(freq_slot[:, None] * blocks[None, :], slot_count)
    block_cos = jnp.cos(block_phase)
    block_sin = jnp.sin(block_phase)
    local_ids = jnp.arange(local_rows, dtype=jnp.int32)
    local_time = local_ids // per_peer * row_count + position * per_peer + local_ids % per_peer
    twist_angle = -angles(freq_slot[:, None] * local_time[None, :], length)
    twist_cos = jnp.cos(twist_angle)[:, :, None]
    twist_sin = jnp.sin(twist_angle)[:, :, None]

    def forward_blocks(real_part):
        out_real = contract("jd,dmc->jmc", block_cos, real_part)
        out_imag = -contract("jd,dmc->jmc", block_sin, real_part)
        return jnp.stack(
            [
                out_real * twist_cos - out_imag * twist_sin,
                out_real * twist_sin + out_imag * twist_cos,
            ]
        )

    all_ids = jnp.arange(tokens, dtype=jnp.int32)
    peer_id = all_ids // local_rows
    within = all_ids % local_rows
    all_time = within // per_peer * row_count + peer_id * per_peer + within % per_peer
    inner_phase = angles(all_ids[:, None] * all_time[None, :], tokens)
    inner_cos = jnp.cos(inner_phase)
    inner_sin = jnp.sin(inner_phase)

    def forward_inner(spectrum):
        real_part = spectrum[0]
        imag_part = spectrum[1]
        out_real = contract("qp,jpc->jqc", inner_cos, real_part) + contract(
            "qp,jpc->jqc", inner_sin, imag_part
        )
        out_imag = contract("qp,jpc->jqc", inner_cos, imag_part) - contract(
            "qp,jpc->jqc", inner_sin, real_part
        )
        return (out_real, out_imag)

    signal_spectrum, filter_spectrum = (
        lax.all_to_all(
            forward_blocks(moved_signal), "seq", split_axis=1, concat_axis=2, tiled=True
        ),
        lax.all_to_all(
            forward_blocks(moved_filter), "seq", split_axis=1, concat_axis=2, tiled=True
        ),
    )
    signal_real, signal_imag = forward_inner(signal_spectrum)
    filter_real, filter_imag = forward_inner(filter_spectrum)
    product_real = signal_real * filter_real - signal_imag * filter_imag
    product_imag = signal_real * filter_imag + signal_imag * filter_real
    back_real = contract("qp,jqc->jpc", inner_cos, product_real) - contract(
        "qp,jqc->jpc", inner_sin, product_imag
    )
    back_imag = contract("qp,jqc->jpc", inner_cos, product_imag) + contract(
        "qp,jqc->jpc", inner_sin, product_real
    )
    my_slots = jnp.stack([position, jnp.where(position == 0, seq_count, slot_count - position)])
    back_phase = angles(my_slots[:, None] * all_time[None, :], length)[:, :, None]
    back_cos = jnp.cos(back_phase)
    back_sin = jnp.sin(back_phase)
    turned_real = back_real * back_cos - back_imag * back_sin
    turned_imag = back_real * back_sin + back_imag * back_cos
    inverse_scale = 1.0 / length
    gathered = lax.all_to_all(
        jnp.stack([turned_real, turned_imag]), "seq", split_axis=2, concat_axis=1, tiled=True
    )
    convolved = (
        contract("jd,jmc->dmc", block_cos, gathered[0])
        - contract("jd,jmc->dmc", block_sin, gathered[1])
    ) * inverse_scale
    returned = lax.all_to_all(
        lax.all_to_all(
            convolved.reshape(seq_count, 1, group_count, per_peer, columns),
            "seq",
            split_axis=0,
            concat_axis=1,
            tiled=True,
        ),
        "ch",
        split_axis=2,
        concat_axis=4,
        tiled=True,
    )
    convolved_rows = returned.reshape(row_count, full_width)
    gated = query_rows.astype(jnp.float32) * (convolved_rows + skip_gain[None, :] * signal)
    return gated.astype(jnp.bfloat16)


def solution(mesh):
    in_specs = (
        P(("seq", "ch"), None),
        P(("seq", "ch"), None),
        P(("seq", "ch"), None),
        P(("seq", "ch"), None),
        P(),
    )
    out_specs = P(("seq", "ch"), None)
    return jax.shard_map(shards, mesh=mesh, in_specs=in_specs, out_specs=out_specs, check_vma=False)
```

profile of v0, /device:TPU:0, one launch (start us, length us, event | category | flops | bytes accessed | tf_op | source)
XLA Modules:
  0.0 577.8 jit_solution(11160475574549039905)
XLA Ops:
  0.0 7.4 %all-to-all-start.3 = ((f32[1,8,1,8,4096]{4,3,2,0,1:T(8,128)}), f32[1,8,1,8,4096]{4,3,2,0,1:T(8,128)S(1)}, u32[]{:S(2)}, u32[]{:S(2)}) async-start(f32[1,8,1,8,4096]{4,3,2,0,1:T(8,128)} %bitcast.167), calls=%async_computation.3 | async-start | bytes 2097152 | tf_op jit(solution)/shard_map/all_to_all | solution.py:42
  7.4 1.1 fusion.15
  8.5 24.7 %all-to-all-done.3 = f32[1,8,1,8,4096]{4,3,2,0,1:T(8,128)S(1)} async-done(((f32[1,8,1,8,4096]{4,3,2,0,1:T(8,128)}), f32[1,8,1,8,4096]{4,3,2,0,1:T(8,128)S(1)}, u32[]{:S(2)}, u32[]{:S(2)}) %all-to-all-start.3) | async-done | bytes 1048608 | tf_op jit(solution)/shard_map/all_to_all | solution.py:42
  33.2 3.6 all-to-all-start
  36.8 8.7 %copy.61 = f32[8,1,1,8,4096]{3,0,2,1,4:T(8,128)} copy(f32[8,1,1,8,4096]{4,3,0,2,1:T(8,128)S(1)} %bitcast.159) | data formatting | bytes 2097152 | tf_op jit(solution)/shard_map/all_to_all | solution.py:42
  45.5 11.9 %reshape.292 = f32[4,1,65536]{2,1,0:T(1,128)} reshape(f32[4096,1,1,8,8]{4,3,2,1,0:T(8,128)} %bitcast.139) | data formatting | bytes 2097152
  57.4 5.3 all-to-all-done
  62.7 3.5 all-to-all-start.4
  66.3 8.7 %copy.52 = f32[8,1,1,8,4096]{3,0,2,1,4:T(8,128)} copy(f32[8,1,1,8,4096]{4,3,0,2,1:T(8,128)S(1)} %bitcast.158) | data formatting | bytes 2097152 | tf_op jit(solution)/shard_map/all_to_all | solution.py:35
  75.0 11.9 %reshape.290 = f32[4,1,65536]{2,1,0:T(1,128)} reshape(f32[4096,1,1,8,8]{4,3,2,1,0:T(8,128)} %bitcast.140) | data formatting | bytes 2097152
  86.9 4.7 all-to-all-start.1
  92.3 3.7 reduce
  96.0 14.8 %reshape.293 = f32[4096,1,1,8,8]{4,3,2,1,0:T(8,128)} reshape(f32[4,65536]{1,0:T(4,128)S(1)} %reduce) | data formatting | bytes 2097152
  110.8 10.0 %copy.90 = f32[8,1,1,8,4,1024]{5,4,3,0,2,1:T(4,128)S(1)} copy(f32[8,1,1,8,4,1024]{3,0,5,4,2,1:T(8,128)} %bitcast.141) | data formatting | bytes 2097152 | tf_op jit(solution)/shard_map/all_to_all | solution.py:41
  120.8 0.6 copy.63
  121.4 1.9 fusion.62
  123.3 3.2 fusion.68
  126.6 4.6 reduce.1
  131.2 15.0 %reshape.291 = f32[4096,1,1,8,8]{4,3,2,1,0:T(8,128)} reshape(f32[4,65536]{1,0:T(4,128)S(1)} %reduce.1) | data formatting | bytes 2097152
  146.2 9.8 %copy.89 = f32[8,1,1,8,4,1024]{5,4,3,0,2,1:T(4,128)S(1)} copy(f32[8,1,1,8,4,1024]{3,0,5,4,2,1:T(8,128)} %bitcast.142) | data formatting | bytes 2097152 | tf_op jit(solution)/shard_map/all_to_all | solution.py:34
  156.0 0.6 copy.54
  156.7 1.9 fusion.64
  158.6 4.8 subtract_bitcast_fusion.1
  164.0 4.4 copy.64
  168.4 4.7 all-to-all-start.5
  173.1 2.0 pad_maximum_fusion
  175.1 4.4 copy.55
  179.6 87.6 %all-to-all-done.5 = f32[2,16,32,1024]{3,2,0,1:T(8,128)} async-done(((f32[2,16,32,1024]{3,2,0,1:T(8,128)}), f32[2,16,32,1024]{3,2,0,1:T(8,128)}, u32[]{:S(2)}, u32[]{:S(2)}) %all-to-all-start.5) | async-done | bytes 4194336 | tf_op jit(solution)/shard_map/all_to_all | solution.py:101
  267.2 5.0 all-to-all-start.2
  272.4 2.5 copy.65
  274.9 0.6 fusion.169
  276.0 4.4 fusion.31
  280.5 5.8 %fusion.27 = f32[2,1024,256]{2,1,0:T(8,128)} fusion(f32[2,256,1024]{2,1,0:T(8,128)S(1)} %bitcast.145, s32[256]{0:T(256)S(1)} %fusion.88), kind=kOutput, calls=%fused_computation.45 | convolution fusion | flops 1611530240 | bytes 4195328 | tf_op jit(solution)/shard_map/qp,jpc->jqc/dot_general | solution.py:15
  286.3 6.0 %convolution_add_fusion = f32[2,1024,256]{2,1,0:T(8,128)} fusion(f32[2,1024,256]{2,1,0:T(8,128)S(1)} %fusion.31, f32[2,256,1024]{2,1,0:T(8,128)S(1)} %bitcast.146, s32[256]{0:T(256)S(1)} %fusion.88), kind=kOutput, calls=%fused_computation.23 | convolution fusion | flops 1612054528 | bytes 6292480 | tf_op jit(solution)/shard_map/qp,jpc->jqc/dot_general | solution.py:15
  292.3 72.9 %all-to-all-done.2 = f32[2,16,32,1024]{3,2,0,1:T(8,128)} async-done(((f32[2,16,32,1024]{3,2,0,1:T(8,128)}), f32[2,16,32,1024]{3,2,0,1:T(8,128)}, u32[]{:S(2)}, u32[]{:S(2)}) %all-to-all-start.2) | async-done | bytes 4194336 | tf_op jit(solution)/shard_map/all_to_all | solution.py:98
  365.1 2.5 copy.56
  367.6 0.6 fusion.170
  368.5 4.4 fusion.33
  373.1 4.5 fusion.29
  377.6 4.7 convolution_add_fusion.1
  382.4 4.3 convolution_subtract_fusion
  386.7 5.0 multiply_subtract_fusion
  391.7 2.8 fusion.2
  394.6 2.8 fusion
  397.4 2.8 fusion.8
  400.3 3.4 subtract_bitcast_fusion
  403.6 2.2 pad_maximum_fusion.2
  405.8 7.4 %copy.74 = f32[2,2,256,1024]{3,1,0,2:T(2,128)} copy(f32[2,2,256,1024]{2,3,1,0:T(8,128)} %pad_maximum_fusion.2) | data formatting | bytes 8388608 | tf_op jit(solution)/shard_map/stack | solution.py:123
  413.3 96.9 %all_to_all.126 = f32[2,2,256,1024]{3,1,0,2:T(2,128)S(1)} all-to-all(f32[2,2,256,1024]{3,1,0,2:T(2,128)} %copy.74), channel_id=1, replica_groups=mesh['seq'=8,'ch'=4] {'seq'}, dimensions={2} | all-to-all | bytes 8388608 | tf_op jit(solution)/shard_map/all_to_all | solution.py:122
  510.2 2.4 copy.75
  512.6 1.8 fusion.168
  514.4 1.6 copy.76
  516.0 2.4 squeeze.22
  518.5 2.9 fusion.66
  521.4 3.0 copy.77
  524.3 2.7 squeeze.23
  527.0 1.1 fusion.14
  528.2 0.6 copy.78
  528.8 28.9 %all_to_all.127 = f32[8,1,4,8,1024]{4,3,2,1,0:T(8,128)S(1)} all-to-all(f32[8,1,4,8,1024]{4,3,2,1,0:T(8,128)S(1)} %copy.78), channel_id=1, replica_groups=mesh['seq'=8,'ch'=4] {'seq'}, dimensions={0} | all-to-all | bytes 2097152 | tf_op jit(solution)/shard_map/all_to_all | solution.py:130
  557.7 0.6 copy.79
  558.3 16.9 %all_to_all.128 = f32[1,8,4,8,1024]{4,1,3,0,2:T(8,128)S(1)} all-to-all(f32[1,8,4,8,1024]{4,1,3,0,2:T(8,128)S(1)} %copy.79), channel_id=1, replica_groups=mesh['seq'=8,'ch'=4] {'ch'}, dimensions={2} | all-to-all | bytes 2097152 | tf_op jit(solution)/shard_map/all_to_all | solution.py:129
  575.2 0.7 copy.93
  575.9 0.6 copy.91
  576.5 1.1 multiply_convert_fusion
  (36 shorter events, 2.5 us)
Async XLA Ops:
  0.0 7.4 %copy-start.7 = (bf16[64,4096]{1,0:T(8,128)(2,1)S(1)}, bf16[64,4096]{1,0:T(8,128)(2,1)}, u32[]{:S(2)}) copy-start(bf16[64,4096]{1,0:T(8,128)(2,1)} %param.6) | copy-start | bytes 1572868
  0.0 7.4 %copy-start.5 = (bf16[64,4096]{1,0:T(8,128)(2,1)S(1)}, bf16[64,4096]{1,0:T(8,128)(2,1)}, u32[]{:S(2)}) copy-start(bf16[64,4096]{1,0:T(8,128)(2,1)} %param.7) | copy-start | bytes 1572868
  0.0 33.2 %all-to-all-start.3 = ((f32[1,8,1,8,4096]{4,3,2,0,1:T(8,128)}), f32[1,8,1,8,4096]{4,3,2,0,1:T(8,128)S(1)}, u32[]{:S(2)}, u32[]{:S(2)}) async-start(f32[1,8,1,8,4096]{4,3,2,0,1:T(8,128)} %bitcast.167), calls=%async_computation.3 | async-start | bytes 2097152 | tf_op jit(solution)/shard_map/all_to_all | solution.py:42
  33.2 29.5 %all-to-all-start = ((f32[1,8,1,8,4096]{4,3,2,0,1:T(8,128)}), f32[1,8,1,8,4096]{4,3,2,0,1:T(8,128)S(1)}, u32[]{:S(2)}, u32[]{:S(2)}) async-start(f32[1,8,1,8,4096]{4,3,2,0,1:T(8,128)} %fusion.15), calls=%async_computation | async-start | bytes 2097152 | tf_op jit(solution)/shard_map/all_to_all | solution.py:35
  62.7 24.2 %all-to-all-start.4 = ((f32[4,1,65536]{2,1,0:T(1,128)}), f32[4,1,65536]{2,1,0:T(1,128)S(1)}, u32[]{:S(2)}, u32[]{:S(2)}) async-start(f32[4,1,65536]{2,1,0:T(1,128)} %reshape.292), calls=%async_computation.4 | async-start | bytes 2097152 | tf_op jit(solution)/shard_map/all_to_all | solution.py:41
  86.9 39.6 %all-to-all-start.1 = ((f32[4,1,65536]{2,1,0:T(1,128)}), f32[4,1,65536]{2,1,0:T(1,128)}, u32[]{:S(2)}, u32[]{:S(2)}) async-start(f32[4,1,65536]{2,1,0:T(1,128)} %reshape.290), calls=%async_computation.1 | async-start | bytes 2097152 | tf_op jit(solution)/shard_map/all_to_all | solution.py:34
  156.6 1.9 copy-start
  168.4 4.7 copy-start.2
  168.4 98.8 %all-to-all-start.5 = ((f32[2,16,32,1024]{3,2,0,1:T(8,128)}), f32[2,16,32,1024]{3,2,0,1:T(8,128)}, u32[]{:S(2)}, u32[]{:S(2)}) async-start(f32[2,16,32,1024]{3,2,0,1:T(8,128)} %copy.64), calls=%async_computation.5 | async-start | bytes 8388608 | tf_op jit(solution)/shard_map/all_to_all | solution.py:101
  267.2 97.9 %all-to-all-start.2 = ((f32[2,16,32,1024]{3,2,0,1:T(8,128)}), f32[2,16,32,1024]{3,2,0,1:T(8,128)}, u32[]{:S(2)}, u32[]{:S(2)}) async-start(f32[2,16,32,1024]{3,2,0,1:T(8,128)} %copy.55), calls=%async_computation.2 | async-start | bytes 8388608 | tf_op jit(solution)/shard_map/all_to_all | solution.py:98
  377.6 4.7 copy-start.1
  382.4 4.3 copy-start.4
  518.5 2.9 copy-start.3
  575.2 1.3 copy-start.6
  575.2 1.3 copy-start.8
  575.2 1.4 copy-start.9
  575.2 1.4 copy-start.10
where the time goes:
time: 584 us; the launch traced here: 578 us
  waiting for transfers between devices  190 us (33%)
  blocking collectives  143 us (24%)
  local copies, waits for them, and re-layouts  133 us (23%)
  matrix products  66.9 us (11%)
  starting transfers between devices  28.9 us (5%)
  other arithmetic  15.6 us (3%)
    all_to_all x1, blocking collectives, shards(): lax.all_to_all(jnp.stack([turned_real, turned_imag]), 'seq', split_axis=2...  96.9 us
    all_to_all x1, waiting for transfers between devices, shards(): lax.all_to_all(forward_blocks(moved_filter), 'seq', split_axis=1, concat_...  87.6 us
    all_to_all x1, waiting for transfers between devices, shards(): lax.all_to_all(forward_blocks(moved_signal), 'seq', split_axis=1, concat_...  72.9 us
    dot_general x18, matrix products, contract(): jnp.einsum(pattern, weights, operand, precision=highest, preferred_elemen...  66.9 us
    unnamed x27, local copies, waits for them, and re-layouts  54.3 us
    all_to_all x1, blocking collectives, shards(): lax.all_to_all(convolved.reshape(seq_count, 1, group_count, per_peer, col...  28.9 us
    all_to_all x1, waiting for transfers between devices, shards(): lax.all_to_all(filter_taps.reshape(layout), 'seq', split_axis=1, concat_a...  24.7 us
    all_to_all x1, blocking collectives, shards(): lax.all_to_all(lax.all_to_all(convolved.reshape(seq_count, 1, group_count...  16.9 us
  transfers between devices with their start and end apart: 6, of which 4 were waited for; matrix products, arithmetic and copies ran while one was open for 18% of the time, Pallas kernels for 0%

commit v1 on v0

--- a/solution.py
+++ b/solution.py
@@ -30,6 +30,27 @@
     length = 2 * tokens * seq_count
     signal = key_rows.astype(jnp.float32) * value_rows.astype(jnp.float32)
     layout = (1, seq_count, 1, per_peer, full_width)
+
+    def change_the_masks(row_data):
+        top = lax.psum(1, "ch")
+        opened = lax.axis_index("ch")
+        t_next, before = (top, opened)
+        out_arr = row_data.shape[4] // t_next
+        prior = list(row_data.shape)
+        prior[4] = out_arr
+        r_now = prior[2]
+        prior[2] = r_now * t_next
+        z1 = jnp.zeros(prior, row_data.dtype)
+        for ix in [*range(t_next)]:
+            part_now = lax.dynamic_slice_in_dim(row_data, (before ^ ix) * out_arr, out_arr, axis=4)
+            if ix:
+                shelf = []
+                for at in [*range(t_next)]:
+                    shelf.append((at, at ^ ix))
+                part_now = lax.ppermute(part_now, "ch", shelf)
+            z1 = lax.dynamic_update_slice_in_dim(z1, part_now, (before ^ ix) * r_now, axis=2)
+        return z1
+
     moved_signal, moved_filter = (
         lax.all_to_all(
             lax.all_to_all(signal.reshape(layout), "seq", split_axis=1, concat_axis=0, tiled=True),
@@ -38,14 +59,10 @@
             concat_axis=2,
             tiled=True,
         ),
-        lax.all_to_all(
+        change_the_masks(
             lax.all_to_all(
                 filter_taps.reshape(layout), "seq", split_axis=1, concat_axis=0, tiled=True
-            ),
-            "ch",
-            split_axis=4,
-            concat_axis=2,
-            tiled=True,
+            )
         ),
     )
     moved_signal = moved_signal.reshape(seq_count, local_rows, columns)

time: 584 us -> 565 us (0.967)
  local copies, waits for them, and re-layouts: 133 us -> 91.4 us
  waiting for transfers between devices: 190 us -> 219 us
    unnamed x27 -> x23, local copies, waits for them, and re-layouts: 54.3 us -> 29.4 us
    all_to_all x4 -> x0, local copies, waits for them, and re-layouts: 19.9 us -> none  [the longest x3 11.1 us: shards(): lax.all_to_all(lax.all_to_all(filter_taps.reshape(layout), 'seq', split_a...]
    all_to_all x1, waiting for transfers between devices: 5.3 us -> 23.6 us  [shards(): lax.all_to_all(signal.reshape(layout), 'seq', split_axis=1, concat_axis=0...]
    all_to_all x1, waiting for transfers between devices: 0.01 us -> 11.8 us  [shards(): lax.all_to_all(lax.all_to_all(signal.reshape(layout), 'seq', split_axis=1...]
    all_to_all x2 -> x3, local copies, waits for them, and re-layouts: 10.5 us -> 13.1 us  [shards(): lax.all_to_all(lax.all_to_all(signal.reshape(layout), 'seq', split_axis=1...]
  transfers between devices with their start and end apart: 6 -> 8, of which waited for: 4 -> 5; matrix products, arithmetic and copies ran while one was open for 18% -> 9% of each run, Pallas kernels for 0% -> 0%
where the time goes in v1:
time: 565 us; the launch traced here: 560 us
  waiting for transfers between devices  219 us (39%)
  blocking collectives  143 us (25%)
  local copies, waits for them, and re-layouts  91.4 us (16%)
  matrix products  66.6 us (12%)
  starting transfers between devices  27.2 us (5%)
  other arithmetic  12.9 us (2%)
    all_to_all x1, blocking collectives, shards(): lax.all_to_all(jnp.stack([turned_real, turned_imag]), 'seq', split_axis=2...  96.9 us
    all_to_all x1, waiting for transfers between devices, shards(): lax.all_to_all(forward_blocks(moved_filter), 'seq', split_axis=1, concat_...  86.8 us
    all_to_all x1, waiting for transfers between devices, shards(): lax.all_to_all(forward_blocks(moved_signal), 'seq', split_axis=1, concat_...  71.9 us
    dot_general x18, matrix products, contract(): jnp.einsum(pattern, weights, operand, precision=highest, preferred_elemen...  66.6 us
    unnamed x23, local copies, waits for them, and re-layouts  29.4 us
    all_to_all x1, blocking collectives, shards(): lax.all_to_all(convolved.reshape(seq_count, 1, group_count, per_peer, col...  28.9 us
    all_to_all x1, waiting for transfers between devices, shards(): lax.all_to_all(filter_taps.reshape(layout), 'seq', split_axis=1, concat_a...  24.7 us
    all_to_all x1, waiting for transfers between devices, shards(): lax.all_to_all(signal.reshape(layout), 'seq', split_axis=1, concat_axis=0...  23.6 us
  transfers between devices with their start and end apart: 8, of which 5 were waited for; matrix products, arithmetic and copies ran while one was open for 9% of the time, Pallas kernels for 0%

profile of v1, /device:TPU:0, one launch (start us, length us, event | category | flops | bytes accessed | tf_op | source)
XLA Modules:
  0.0 560.2 jit_solution(16858539066623607611)
XLA Ops:
  0.0 7.4 %all-to-all-start.3 = ((f32[1,8,1,8,4096]{4,3,2,0,1:T(8,128)}), f32[1,8,1,8,4096]{4,3,2,0,1:T(8,128)S(1)}, u32[]{:S(2)}, u32[]{:S(2)}) async-start(f32[1,8,1,8,4096]{4,3,2,0,1:T(8,128)} %bitcast.171), calls=%async_computation.3 | async-start | bytes 2097152 | tf_op jit(solution)/shard_map/all_to_all | solution.py:63
  7.4 1.1 fusion.15
  8.5 24.7 %all-to-all-done.3 = f32[1,8,1,8,4096]{4,3,2,0,1:T(8,128)S(1)} async-done(((f32[1,8,1,8,4096]{4,3,2,0,1:T(8,128)}), f32[1,8,1,8,4096]{4,3,2,0,1:T(8,128)S(1)}, u32[]{:S(2)}, u32[]{:S(2)}) %all-to-all-start.3) | async-done | bytes 1048608 | tf_op jit(solution)/shard_map/all_to_all | solution.py:63
  33.2 3.6 all-to-all-start
  37.2 1.6 collective-permute-start.1
  38.7 0.4 collective-permute-start.2
  39.1 23.6 %all-to-all-done = f32[1,8,1,8,4096]{4,3,2,0,1:T(8,128)S(1)} async-done(((f32[1,8,1,8,4096]{4,3,2,0,1:T(8,128)}), f32[1,8,1,8,4096]{4,3,2,0,1:T(8,128)S(1)}, u32[]{:S(2)}, u32[]{:S(2)}) %all-to-all-start) | async-done | bytes 1048608 | tf_op jit(solution)/shard_map/all_to_all | solution.py:56
  62.7 8.8 %copy.60 = f32[8,1,1,8,4096]{3,0,2,1,4:T(8,128)} copy(f32[8,1,1,8,4096]{4,3,0,2,1:T(8,128)S(1)} %bitcast.163) | data formatting | bytes 2097152 | tf_op jit(solution)/shard_map/all_to_all | solution.py:56
  71.5 11.9 %reshape.295 = f32[4,1,65536]{2,1,0:T(1,128)} reshape(f32[4096,1,1,8,8]{4,3,2,1,0:T(8,128)} %bitcast.146) | data formatting | bytes 2097152
  83.4 4.4 all-to-all-start.1
  88.7 1.9 fusion.62
  90.6 11.8 %all-to-all-done.1 = f32[4,1,65536]{2,1,0:T(1,128)} async-done(((f32[4,1,65536]{2,1,0:T(1,128)}), f32[4,1,65536]{2,1,0:T(1,128)}, u32[]{:S(2)}, u32[]{:S(2)}) %all-to-all-start.1) | async-done | bytes 1048608 | tf_op jit(solution)/shard_map/all_to_all | solution.py:55
  102.3 0.5 broadcast.519
  102.8 5.5 reduce
  108.3 16.8 %reshape.296 = f32[4096,1,1,8,8]{4,3,2,1,0:T(8,128)} reshape(f32[4,65536]{1,0:T(4,128)} %reduce) | data formatting | bytes 2097152
  125.2 10.8 %copy.102 = f32[8,1,1,8,4,1024]{5,4,3,0,2,1:T(4,128)} copy(f32[8,1,1,8,4,1024]{3,0,5,4,2,1:T(8,128)} %bitcast.147) | data formatting | bytes 2097152 | tf_op jit(solution)/shard_map/all_to_all | solution.py:55
  136.0 1.8 copy.62
  137.8 1.9 fusion.64
  139.7 1.9 fusion.70
  141.6 5.9 %subtract_bitcast_fusion.1 = (f32[1,16,32,1024]{3,1,2,0:T(8,128)S(1)}, f32[1,16,32,1024]{3,1,2,0:T(8,128)S(1)}, f32[1,16,32,1024]{3,1,2,0:T(8,128)}, f32[1,16,32,1024]{3,1,2,0:T(8,128)}) fusion(f32[16,32,1024]{2,0,1:T(8,128)S(1)} %fusion.62, f32[16,32]{0,1:T(8,128)S(1)} %get-tuple-element.28, f32[16,32]{0,1:T(8,128)S(1)} %get-tuple-element.27, ...), kind=kOutput, calls=%fused_computation.16 | convolution fusion | flops 57673472 | bytes 15732800 | tf_op jit(solution)/shard_map/jd,dmc->jmc/dot_general | solution.py:15
  147.4 0.6 pad_maximum_fusion.1
  148.0 4.4 copy.77
  152.4 4.7 all-to-all-start.4
  157.2 2.0 pad_maximum_fusion
  159.2 4.5 copy.63
  163.6 86.8 %all-to-all-done.4 = f32[2,16,32,1024]{3,2,0,1:T(8,128)} async-done(((f32[2,16,32,1024]{3,2,0,1:T(8,128)}), f32[2,16,32,1024]{3,2,0,1:T(8,128)}, u32[]{:S(2)}, u32[]{:S(2)}) %all-to-all-start.4) | async-done | bytes 4194336 | tf_op jit(solution)/shard_map/all_to_all | solution.py:118
  250.4 5.1 all-to-all-start.2
  255.7 2.5 copy.78
  258.2 0.6 fusion.169
  258.8 0.2 copy.79
  259.1 0.2 copy.81
  259.3 4.4 fusion.31
  263.7 5.8 %fusion.27 = f32[2,1024,256]{2,1,0:T(8,128)} fusion(f32[2,256,1024]{2,1,0:T(8,128)S(1)} %bitcast.150, s32[256]{0:T(256)S(1)} %fusion.106), kind=kOutput, calls=%fused_computation.45 | convolution fusion | flops 1611530240 | bytes 4195328 | tf_op jit(solution)/shard_map/qp,jpc->jqc/dot_general | solution.py:15
  269.5 6.0 %convolution_add_fusion = f32[2,1024,256]{2,1,0:T(8,128)} fusion(f32[2,1024,256]{2,1,0:T(8,128)S(1)} %fusion.31, f32[2,256,1024]{2,1,0:T(8,128)S(1)} %bitcast.151, s32[256]{0:T(256)S(1)} %fusion.106), kind=kOutput, calls=%fused_computation.23 | convolution fusion | flops 1612054528 | bytes 6292480 | tf_op jit(solution)/shard_map/qp,jpc->jqc/dot_general | solution.py:15
  275.6 71.9 %all-to-all-done.2 = f32[2,16,32,1024]{3,2,0,1:T(8,128)} async-done(((f32[2,16,32,1024]{3,2,0,1:T(8,128)}), f32[2,16,32,1024]{3,2,0,1:T(8,128)}, u32[]{:S(2)}, u32[]{:S(2)}) %all-to-all-start.2) | async-done | bytes 4194336 | tf_op jit(solution)/shard_map/all_to_all | solution.py:115
  347.5 2.5 copy.64
  350.0 0.6 fusion.170
  350.8 4.4 fusion.33
  355.5 4.5 fusion.29
  360.0 4.7 convolution_add_fusion.1
  364.7 4.3 convolution_subtract_fusion
  369.1 5.0 multiply_subtract_fusion
  374.1 2.8 fusion.2
  376.9 2.8 fusion
  379.8 2.9 fusion.8
  382.7 3.3 subtract_bitcast_fusion
  386.1 2.2 pad_maximum_fusion.2
  388.3 7.4 %copy.87 = f32[2,2,256,1024]{3,1,0,2:T(2,128)} copy(f32[2,2,256,1024]{2,3,1,0:T(8,128)} %pad_maximum_fusion.2) | data formatting | bytes 8388608 | tf_op jit(solution)/shard_map/stack | solution.py:140
  395.7 96.9 %all_to_all.108 = f32[2,2,256,1024]{3,1,0,2:T(2,128)S(1)} all-to-all(f32[2,2,256,1024]{3,1,0,2:T(2,128)} %copy.87), channel_id=1, replica_groups=mesh['seq'=8,'ch'=4] {'seq'}, dimensions={2} | all-to-all | bytes 8388608 | tf_op jit(solution)/shard_map/all_to_all | solution.py:139
  492.7 2.4 copy.88
  495.1 1.8 fusion.168
  496.9 1.6 copy.89
  498.5 2.4 squeeze.22
  500.9 2.9 fusion.66
  503.8 3.0 copy.90
  506.8 2.7 squeeze.23
  509.5 1.1 fusion.14
  510.6 0.6 copy.91
  511.2 28.9 %all_to_all.109 = f32[8,1,4,8,1024]{4,3,2,1,0:T(8,128)S(1)} all-to-all(f32[8,1,4,8,1024]{4,3,2,1,0:T(8,128)S(1)} %copy.91), channel_id=1, replica_groups=mesh['seq'=8,'ch'=4] {'seq'}, dimensions={0} | all-to-all | bytes 2097152 | tf_op jit(solution)/shard_map/all_to_all | solution.py:147
  540.1 0.6 copy.92
  540.8 16.9 %all_to_all.110 = f32[1,8,4,8,1024]{4,1,3,0,2:T(8,128)S(1)} all-to-all(f32[1,8,4,8,1024]{4,1,3,0,2:T(8,128)S(1)} %copy.92), channel_id=1, replica_groups=mesh['seq'=8,'ch'=4] {'ch'}, dimensions={2} | all-to-all | bytes 2097152 | tf_op jit(solution)/shard_map/all_to_all | solution.py:146
  557.6 0.7 copy.109
  558.3 0.6 copy.103
  559.0 1.1 multiply_convert_fusion
  (38 shorter events, 1.9 us)
Async XLA Ops:
  0.0 7.4 %copy-start.6 = (bf16[64,4096]{1,0:T(8,128)(2,1)S(1)}, bf16[64,4096]{1,0:T(8,128)(2,1)}, u32[]{:S(2)}) copy-start(bf16[64,4096]{1,0:T(8,128)(2,1)} %param.6) | copy-start | bytes 1572868
  0.0 7.4 %copy-start.4 = (bf16[64,4096]{1,0:T(8,128)(2,1)S(1)}, bf16[64,4096]{1,0:T(8,128)(2,1)}, u32[]{:S(2)}) copy-start(bf16[64,4096]{1,0:T(8,128)(2,1)} %param.7) | copy-start | bytes 1572868
  0.0 33.2 %all-to-all-start.3 = ((f32[1,8,1,8,4096]{4,3,2,0,1:T(8,128)}), f32[1,8,1,8,4096]{4,3,2,0,1:T(8,128)S(1)}, u32[]{:S(2)}, u32[]{:S(2)}) async-start(f32[1,8,1,8,4096]{4,3,2,0,1:T(8,128)} %bitcast.171), calls=%async_computation.3 | async-start | bytes 2097152 | tf_op jit(solution)/shard_map/all_to_all | solution.py:63
  33.2 29.5 %all-to-all-start = ((f32[1,8,1,8,4096]{4,3,2,0,1:T(8,128)}), f32[1,8,1,8,4096]{4,3,2,0,1:T(8,128)S(1)}, u32[]{:S(2)}, u32[]{:S(2)}) async-start(f32[1,8,1,8,4096]{4,3,2,0,1:T(8,128)} %fusion.15), calls=%async_computation | async-start | bytes 2097152 | tf_op jit(solution)/shard_map/all_to_all | solution.py:56
  36.9 51.2 %collective-permute-start = (f32[8,1,1,8,1024]{4,3,0,2,1:T(8,128)S(1)}, f32[8,1,1,8,1024]{4,3,0,2,1:T(8,128)S(1)}, u32[]{:S(2)}, u32[]{:S(2)}) collective-permute-start(f32[8,1,1,8,1024]{4,3,0,2,1:T(8,128)S(1)} %get-tuple-element.21), channel_id=1, source_target_pairs={{0,1},{1,0},{2,3},{3,2},{4,5},{5,4},{6,7},{7,6},{8,9},{9,8},{10,11... | collective-permute-start | bytes 786440 | tf_op jit(solution)/shard_map/ppermute | solution.py:50
  37.2 51.1 %collective-permute-start.1 = (f32[8,1,1,8,1024]{4,3,0,2,1:T(8,128)S(1)}, f32[8,1,1,8,1024]{4,3,0,2,1:T(8,128)S(1)}, u32[]{:S(2)}, u32[]{:S(2)}) collective-permute-start(f32[8,1,1,8,1024]{4,3,0,2,1:T(8,128)S(1)} %get-tuple-element.20), channel_id=1, source_target_pairs={{0,2},{1,3},{2,0},{3,1},{4,6},{5,7},{6,4},{7,5},{8,10},{9,11},{10,... | collective-permute-start | bytes 786440 | tf_op jit(solution)/shard_map/ppermute | solution.py:50
  38.7 49.7 %collective-permute-start.2 = (f32[8,1,1,8,1024]{4,3,0,2,1:T(8,128)S(1)}, f32[8,1,1,8,1024]{4,3,0,2,1:T(8,128)S(1)}, u32[]{:S(2)}, u32[]{:S(2)}) collective-permute-start(f32[8,1,1,8,1024]{4,3,0,2,1:T(8,128)S(1)} %get-tuple-element.19), channel_id=1, source_target_pairs={{0,3},{1,2},{2,1},{3,0},{4,7},{5,6},{6,5},{7,4},{8,11},{9,10},{10,... | collective-permute-start | bytes 786440 | tf_op jit(solution)/shard_map/ppermute | solution.py:50
  83.4 18.9 %all-to-all-start.1 = ((f32[4,1,65536]{2,1,0:T(1,128)}), f32[4,1,65536]{2,1,0:T(1,128)}, u32[]{:S(2)}, u32[]{:S(2)}) async-start(f32[4,1,65536]{2,1,0:T(1,128)} %reshape.295), calls=%async_computation.1 | async-start | bytes 2097152 | tf_op jit(solution)/shard_map/all_to_all | solution.py:55
  152.4 4.7 copy-start.1
  152.4 98.0 %all-to-all-start.4 = ((f32[2,16,32,1024]{3,2,0,1:T(8,128)}), f32[2,16,32,1024]{3,2,0,1:T(8,128)}, u32[]{:S(2)}, u32[]{:S(2)}) async-start(f32[2,16,32,1024]{3,2,0,1:T(8,128)} %copy.77), calls=%async_computation.4 | async-start | bytes 8388608 | tf_op jit(solution)/shard_map/all_to_all | solution.py:118
  250.4 97.1 %all-to-all-start.2 = ((f32[2,16,32,1024]{3,2,0,1:T(8,128)}), f32[2,16,32,1024]{3,2,0,1:T(8,128)}, u32[]{:S(2)}, u32[]{:S(2)}) async-start(f32[2,16,32,1024]{3,2,0,1:T(8,128)} %copy.63), calls=%async_computation.2 | async-start | bytes 8388608 | tf_op jit(solution)/shard_map/all_to_all | solution.py:115
  360.0 4.7 copy-start
  364.7 4.3 copy-start.3
  500.9 2.9 copy-start.2
  557.6 1.3 copy-start.5
  557.6 1.3 copy-start.7
  557.6 1.4 copy-start.8
  557.6 1.4 copy-start.9
